TPU v7x, 512 devices: a whole 4x4x16 slice. The times are simulated.
512 devices in a mesh: dom: 64 (over x, z), sub: 8 (over y, core).
Axes of the slice: x: 4, y: 4, z: 16, core: 2. Of those that a mesh axis runs over, the one named last changes fastest.
Arguments:
- right_side: float32 [1024, 16, 128], P(('dom', 'sub')), as said below
- diag_blocks: float32 [1024, 128, 128], P(('dom', 'sub')), as said below
- block_values: float32 [1024, 4, 128, 128], P(('dom', 'sub')), as said below
- block_cols: int32 [1024, 4], P(('dom', 'sub')), may hold values from 0 to 31, as said below
- block_count: int32 [1024], P(('dom', 'sub')), may hold values from 0 to 4, as said below
- cell_diagonal: float32 [1024, 128], P(('dom', 'sub')), as said below
Outputs:
- solution_field: float32 [1024, 16, 128], P(('dom', 'sub'))
- residual: float32 [1024, 16, 128], P(('dom', 'sub'))
Inputs may be any that keep to these rules, and one draw needn't show every extreme that they name: `block_cols`: live slots of a block row point to distinct block rows that come after it in the window (positions 0 to 15 are the block rows of the same index of dom, the rest those of the next index); block rows of the last index of dom point only into their own index; dead slots hold 0. `block_count`: the number of live slots, which varies from device to device. `block_values`: entries lie between -1 / 128 and 0. `diag_blocks`: entries lie between -1 / 128 and 0. `cell_diagonal`: every entry exceeds 1 + the live slots of its block row + the live slots of all block rows that couple to its block row, so the operator is strictly diagonally dominant. `right_side`: entries lie between -50 and 50.
All inputs are finite; a program needn't handle non-finite values.
Results may differ from a plain program's by a relative error of at most 0.00065.
Values sent between devices are 32-bit elements; how exact they have to be, the bound alone decides.
A program may use at most 64 MiB of HBM per device.

v0:
```python
import jax
import jax.numpy as jnp
from jax import lax
from jax.sharding import PartitionSpec as P

K = 4
ITERS = 3
PRECISE = lax.Precision.HIGHEST


def passed_along(x, axis, by):
    peers = lax.axis_size(axis)
    pairs = [(i, i + by) for i in range(peers) if 0 <= i + by < peers]
    return lax.ppermute(x, axis, pairs)


def local(right_side, diag_blocks, block_values, block_cols, block_count, cell_diagonal):
    rows_dev = right_side.shape[0]
    group_rows = lax.axis_size("sub") * rows_dev
    upper_part = jnp.triu(diag_blocks, 1)
    live_slots = jnp.arange(K, dtype=jnp.int32)[None, :] < block_count[:, None]
    window_ids = jnp.arange(2 * group_rows, dtype=jnp.int32)
    picker = (
        (block_cols[:, :, None] == window_ids[None, None, :]) & live_slots[:, :, None]
    ).astype(jnp.float32)

    def local_dots(first, second):
        return jnp.sum(first * second, axis=(0, 2))

    def residual_sum(residual_now, precond_now):
        return lax.psum(local_dots(residual_now, precond_now), ("dom", "sub"))

    solution_field = jnp.zeros_like(right_side)
    residual = right_side
    precond_res = residual / cell_diagonal[:, None, :]
    direction = precond_res
    precond_dot = residual_sum(residual, precond_res)
    for iteration in range(ITERS):
        own_part = jnp.einsum("rab,rzb->rza", upper_part, direction, precision=PRECISE)
        own_part = own_part + jnp.einsum("rba,rzb->rza", upper_part, direction, precision=PRECISE)
        own_part = own_part + cell_diagonal[:, None, :] * direction
        own_group = lax.all_gather(direction, "sub", axis=0, tiled=True)
        next_group = passed_along(own_group, "dom", -1)
        window = jnp.concatenate([own_group, next_group], axis=0)
        far_rows = jnp.einsum("rkw,wzb->rkzb", picker, window, precision=PRECISE)
        forward = jnp.einsum("rkab,rkzb->rza", block_values, far_rows, precision=PRECISE)
        back_terms = jnp.einsum("rkba,rzb->rkza", block_values, direction, precision=PRECISE)
        spread = jnp.einsum("rkw,rkza->wza", picker, back_terms, precision=PRECISE)
        incoming = passed_along(spread[group_rows:], "dom", 1)
        back_own = lax.psum_scatter(
            spread[:group_rows] + incoming, "sub", scatter_dimension=0, tiled=True
        )
        image_vec = own_part + forward + back_own
        curvature = lax.psum(local_dots(direction, image_vec), ("dom", "sub"))
        step_size = precond_dot / curvature
        solution_field = solution_field + step_size[None, :, None] * direction
        residual = residual - step_size[None, :, None] * image_vec
        if iteration + 1 < ITERS:
            precond_res = residual / cell_diagonal[:, None, :]
            new_dot = residual_sum(residual, precond_res)
            direction = precond_res + (new_dot / precond_dot)[None, :, None] * direction
            precond_dot = new_dot
    return (solution_field, residual)


def solution(mesh):
    return jax.shard_map(
        local,
        mesh=mesh,
        in_specs=(
            P(("dom", "sub"), None, None),
            P(("dom", "sub"), None, None),
            P(("dom", "sub"), None, None, None),
            P(("dom", "sub"), None),
            P(("dom", "sub")),
            P(("dom", "sub"), None),
        ),
        out_specs=(P(("dom", "sub"), None, None), P(("dom", "sub"), None, None)),
        check_vma=False,
    )
```

profile of v0, /device:TPU:1, one launch (start us, length us, event | category | flops | bytes accessed | tf_op | source)
XLA Modules:
  0.0 715.4 jit_solution(11586665640421009732)
XLA Ops:
  7.2 0.8 broadcast_divide_fusion
  8.0 19.6 %all_gather.9 = f32[16,16,128]{2,1,0:T(8,128)S(1)} all-gather(f32[2,16,128]{2,1,0:T(8,128)S(1)} %broadcast_divide_fusion), channel_id=1, replica_groups=mesh['dom'=64,'sub'=8] {'sub'}, dimensions={0}, use_global_device_ids=true | all-gather | bytes 147456 | tf_op jit(solution)/shard_map/all_gather | solution.py:42
  27.6 1.4 collective-permute-start
  30.3 4.0 collective-permute-start.1
  35.0 1.7 collective-permute-done.1
  36.7 0.7 copy_add_fusion.2
  37.5 0.5 convolution_bitcast_fusion.5
  38.2 37.2 %reduce-scatter.4.cloned.1.call-done = f32[2,16,128]{2,1,0:T(8,128)} async-done(((f32[16,16,128]{2,1,0:T(8,128)}), f32[2,16,128]{2,1,0:T(8,128)}) %reduce-scatter.4.cloned.1.call-update) | async-done | bytes 16400 | tf_op jit(solution)/shard_map/reduce_scatter | solution.py:50
  75.4 0.8 multiply_reduce_fusion.4
  76.2 105.7 %all-reduce = (f32[16]{0:T(128)S(1)}, f32[16]{0:T(128)S(1)}) all-reduce(f32[16]{0:T(128)S(1)} %get-tuple-element.3, f32[16]{0:T(128)S(1)} %get-tuple-element.2), channel_id=1, replica_groups=mesh['dom'=64,'sub'=8] {'dom','sub'}, use_global_device_ids=true, to_apply=%region_1.2 | all-reduce | flops 32 | bytes 256 | tf_op jit(solution)/shard_map/psum | solution.py:31
  182.2 99.4 %psum.44 = f32[16]{0:T(128)S(1)} all-reduce(f32[16]{0:T(128)S(1)} %get-tuple-element.12), channel_id=1, replica_groups=mesh['dom'=64,'sub'=8] {'dom','sub'}, use_global_device_ids=true, to_apply=%region_6.7 | all-reduce | flops 16 | bytes 128 | tf_op jit(solution)/shard_map/psum | solution.py:31
  281.7 13.2 %all_gather.10 = f32[16,16,128]{2,1,0:T(8,128)S(1)} all-gather(f32[2,16,128]{2,1,0:T(8,128)S(1)} %multiply_add_fusion.2), channel_id=1, replica_groups=mesh['dom'=64,'sub'=8] {'sub'}, dimensions={0}, use_global_device_ids=true | all-gather | bytes 147456 | tf_op jit(solution)/shard_map/all_gather | solution.py:42
  295.3 1.3 collective-permute-start.2
  297.1 4.0 collective-permute-start.3
  301.3 0.7 collective-permute-done.2
  302.4 1.0 collective-permute-done.3
  303.4 0.7 copy_add_fusion.1
  304.2 0.5 convolution_bitcast_fusion.4
  305.0 33.6 %reduce-scatter.6.cloned.1.call-done = f32[2,16,128]{2,1,0:T(8,128)} async-done(((f32[16,16,128]{2,1,0:T(8,128)}), f32[2,16,128]{2,1,0:T(8,128)}) %reduce-scatter.6.cloned.1.call-update) | async-done | bytes 16400 | tf_op jit(solution)/shard_map/reduce_scatter | solution.py:50
  338.5 0.8 multiply_reduce_fusion.2
  339.4 105.7 %psum.45 = f32[16]{0:T(128)S(1)} all-reduce(f32[16]{0:T(128)S(1)} %get-tuple-element.10), channel_id=1, replica_groups=mesh['dom'=64,'sub'=8] {'dom','sub'}, use_global_device_ids=true, to_apply=%region_9.10 | all-reduce | flops 16 | bytes 128 | tf_op jit(solution)/shard_map/psum | solution.py:54
  445.3 99.2 %psum.46 = f32[16]{0:T(128)S(1)} all-reduce(f32[16]{0:T(128)S(1)} %get-tuple-element.8), channel_id=1, replica_groups=mesh['dom'=64,'sub'=8] {'dom','sub'}, use_global_device_ids=true, to_apply=%region_11.12 | all-reduce | flops 16 | bytes 128 | tf_op jit(solution)/shard_map/psum | solution.py:31
  544.6 13.2 %all_gather.11 = f32[16,16,128]{2,1,0:T(8,128)S(1)} all-gather(f32[2,16,128]{2,1,0:T(8,128)S(1)} %multiply_add_fusion.1), channel_id=1, replica_groups=mesh['dom'=64,'sub'=8] {'sub'}, dimensions={0}, use_global_device_ids=true | all-gather | bytes 147456 | tf_op jit(solution)/shard_map/all_gather | solution.py:42
  558.2 1.3 collective-permute-start.4
  560.0 4.0 collective-permute-start.5
  564.2 0.7 collective-permute-done.4
  565.3 1.0 collective-permute-done.5
  566.3 0.7 copy_add_fusion
  567.8 33.7 %reduce-scatter.8.cloned.1.call-done = f32[2,16,128]{2,1,0:T(8,128)} async-done(((f32[16,16,128]{2,1,0:T(8,128)}), f32[2,16,128]{2,1,0:T(8,128)}) %reduce-scatter.8.cloned.1.call-update) | async-done | bytes 16400 | tf_op jit(solution)/shard_map/reduce_scatter | solution.py:50
  601.5 0.8 multiply_reduce_fusion
  602.4 105.8 %psum.47 = f32[16]{0:T(128)S(1)} all-reduce(f32[16]{0:T(128)S(1)} %get-tuple-element.6), channel_id=1, replica_groups=mesh['dom'=64,'sub'=8] {'dom','sub'}, use_global_device_ids=true, to_apply=%region_14.15 | all-reduce | flops 16 | bytes 128 | tf_op jit(solution)/shard_map/psum | solution.py:54
  708.2 0.7 multiply_subtract_fusion
  (55 shorter events, 6.7 us)
Async XLA Ops:
  7.2 21.9 %copy-start = (f32[2,4,128,128]{3,2,1,0:T(8,128)S(1)}, f32[2,4,128,128]{3,2,1,0:T(8,128)}, u32[]{:S(2)}) copy-start(f32[2,4,128,128]{3,2,1,0:T(8,128)} %param.8) | copy-start | bytes 1572868
  7.2 68.2 %reduce-scatter.4.cloned.1.call-start = ((), (), s32[]{:S(2)}) async-start(), calls=%async_computation.3 | async-start | bytes 147456 | tf_op jit(solution)/shard_map/reduce_scatter | solution.py:50
  8.0 21.0 %copy-start.5 = (s32[2]{0:T(128)S(1)}, s32[2]{0:T(128)}, u32[]{:S(2)}) copy-start(s32[2]{0:T(128)} %param.10) | copy-start | bytes 28
  8.0 21.1 %copy-start.2 = (f32[2,16,128]{2,1,0:T(8,128)S(1)}, f32[2,16,128]{2,1,0:T(8,128)}, u32[]{:S(2)}) copy-start(f32[2,16,128]{2,1,0:T(8,128)} %param.6) | copy-start | bytes 49156
  27.6 1.5 copy-start.3
  27.6 7.0 collective-permute-start
  29.1 0.7 copy-start.4
  30.2 4.1 copy-start.1
  30.3 6.4 collective-permute-start.1
  37.4 301.1 %reduce-scatter.6.cloned.1.call-start = ((), (), s32[]{:S(2)}) async-start(), calls=%async_computation.4 | async-start | bytes 147456 | tf_op jit(solution)/shard_map/reduce_scatter | solution.py:50
  295.3 6.8 collective-permute-start.2
  297.1 6.4 collective-permute-start.3
  304.2 297.4 %reduce-scatter.8.cloned.1.call-start = ((), (), s32[]{:S(2)}) async-start(), calls=%async_computation.5 | async-start | bytes 147456 | tf_op jit(solution)/shard_map/reduce_scatter | solution.py:50
  558.2 6.8 collective-permute-start.4
  560.0 6.4 collective-permute-start.5
Sparse Core Ops, SparseCore 0:
  37.5 37.8 reduce-scatter.3
  304.3 34.2 reduce-scatter.5
  567.2 34.3 reduce-scatter.7
where the time goes:
time: 717 us; the launch traced here: 715 us
  blocking collectives  562 us (78%)
  waiting for transfers between devices  110 us (15%)
  starting transfers between devices  16.1 us (2%)
  between operations  14 us (2%)
    psum x3, blocking collectives, residual_sum(): return lax.psum(local_dots(residual_now, precond_now), ('dom', 'sub'))  304 us
    psum x2, blocking collectives, local(): curvature = lax.psum(local_dots(direction, image_vec), ('dom', 'sub'))  212 us
    reduce_scatter x3, waiting for transfers between devices, local(): lax.psum_scatter(spread[:group_rows] + incoming, 'sub', scatter_dimension...  104 us
    all_gather x3, blocking collectives, local(): own_group = lax.all_gather(direction, 'sub', axis=0, tiled=True)  46.1 us
    ppermute x6, starting transfers between devices, passed_along(): return lax.ppermute(x, axis, pairs)  16 us
  transfers between devices with their start and end apart: 9, of which 8 were waited for; matrix products, arithmetic and copies ran while one was open for 1% of the time, Pallas kernels for 0%

commit v1 on v0

--- a/solution.py
+++ b/solution.py
@@ -39,7 +39,11 @@
         own_part = jnp.einsum("rab,rzb->rza", upper_part, direction, precision=PRECISE)
         own_part = own_part + jnp.einsum("rba,rzb->rza", upper_part, direction, precision=PRECISE)
         own_part = own_part + cell_diagonal[:, None, :] * direction
-        own_group = lax.all_gather(direction, "sub", axis=0, tiled=True)
+        count = lax.axis_size("sub")
+        repeats = [count if d == 0 else 1 for d in range(direction.ndim)]
+        own_group = lax.all_to_all(
+            jnp.tile(direction, repeats), "sub", split_axis=0, concat_axis=0, tiled=True
+        )
         next_group = passed_along(own_group, "dom", -1)
         window = jnp.concatenate([own_group, next_group], axis=0)
         far_rows = jnp.einsum("rkw,wzb->rkzb", picker, window, precision=PRECISE)

time: 717 us -> 689 us (0.961)
  blocking collectives: 562 us -> 516 us
  starting transfers between devices: 16.1 us -> 28.7 us
    all_gather x3 -> x0, blocking collectives: 46.1 us -> none  [local(): own_group = lax.all_gather(direction, 'sub', axis=0, tiled=True)]
    all_to_all x0 -> x3, starting transfers between devices: none -> 18.2 us  [local(): lax.all_to_all(jnp.tile(direction, repeats), 'sub', split_axis=0, concat_...]
    reduce_scatter x3, waiting for transfers between devices: 104 us -> 94.9 us  [local(): lax.psum_scatter(spread[:group_rows] + incoming, 'sub', scatter_dimension...]
  transfers between devices with their start and end apart: 9 -> 12, of which waited for: 8 -> 9; matrix products, arithmetic and copies ran while one was open for 1% -> 1% of each run, Pallas kernels for 0% -> 0%
where the time goes in v1:
time: 689 us; the launch traced here: 687 us
  blocking collectives  516 us (75%)
  waiting for transfers between devices  112 us (16%)
  starting transfers between devices  28.7 us (4%)
  between operations  14 us (2%)
    psum x3, blocking collectives, residual_sum(): return lax.psum(local_dots(residual_now, precond_now), ('dom', 'sub'))  305 us
    psum x2, blocking collectives, local(): curvature = lax.psum(local_dots(direction, image_vec), ('dom', 'sub'))  211 us
    reduce_scatter x3, waiting for transfers between devices, local(): lax.psum_scatter(spread[:group_rows] + incoming, 'sub', scatter_dimension...  94.9 us
    all_to_all x3, starting transfers between devices, local(): lax.all_to_all(jnp.tile(direction, repeats), 'sub', split_axis=0, concat_...  18.2 us
  transfers between devices with their start and end apart: 12, of which 9 were waited for; matrix products, arithmetic and copies ran while one was open for 1% of the time, Pallas kernels for 0%

profile of v1, /device:TPU:1, one launch (start us, length us, event | category | flops | bytes accessed | tf_op | source)
XLA Modules:
  0.0 687.1 jit_solution(1606716456555195304)
XLA Ops:
  7.2 0.8 broadcast_divide_fusion
  8.0 0.7 tile.12
  8.6 10.3 %all-to-all-start = ((f32[16,16,128]{2,1,0:T(8,128)}), f32[16,16,128]{2,1,0:T(8,128)S(1)}, u32[]{:S(2)}, u32[]{:S(2)}) async-start(f32[16,16,128]{2,1,0:T(8,128)} %bitcast.2), calls=%async_computation | async-start | bytes 262144 | tf_op jit(solution)/shard_map/all_to_all | solution.py:44
  20.8 1.3 collective-permute-start.1
  22.4 1.8 all-to-all-done
  24.2 1.3 collective-permute-start
  25.5 0.7 copy_add_fusion.2
  26.2 4.0 collective-permute-done
  31.3 35.4 %reduce-scatter.4.cloned.1.call-done = f32[2,16,128]{2,1,0:T(8,128)} async-done(((f32[16,16,128]{2,1,0:T(8,128)}), f32[2,16,128]{2,1,0:T(8,128)}) %reduce-scatter.4.cloned.1.call-update) | async-done | bytes 16400 | tf_op jit(solution)/shard_map/reduce_scatter | solution.py:54
  66.7 0.8 multiply_reduce_fusion.4
  67.5 105.8 %all-reduce = (f32[16]{0:T(128)S(1)}, f32[16]{0:T(128)S(1)}) all-reduce(f32[16]{0:T(128)S(1)} %get-tuple-element.3, f32[16]{0:T(128)S(1)} %get-tuple-element.2), channel_id=1, replica_groups=mesh['dom'=64,'sub'=8] {'dom','sub'}, use_global_device_ids=true, to_apply=%region_1.2 | all-reduce | flops 32 | bytes 256 | tf_op jit(solution)/shard_map/psum | solution.py:31
  173.4 99.4 %psum.44 = f32[16]{0:T(128)S(1)} all-reduce(f32[16]{0:T(128)S(1)} %get-tuple-element.12), channel_id=1, replica_groups=mesh['dom'=64,'sub'=8] {'dom','sub'}, use_global_device_ids=true, to_apply=%region_6.7 | all-reduce | flops 16 | bytes 128 | tf_op jit(solution)/shard_map/psum | solution.py:31
  273.9 3.9 all-to-all-start.1
  278.4 2.7 collective-permute-start.3
  281.4 1.8 all-to-all-done.1
  283.2 1.3 collective-permute-start.2
  284.5 0.7 copy_add_fusion.1
  285.2 4.0 collective-permute-done.2
  290.3 29.8 %reduce-scatter.6.cloned.1.call-done = f32[2,16,128]{2,1,0:T(8,128)} async-done(((f32[16,16,128]{2,1,0:T(8,128)}), f32[2,16,128]{2,1,0:T(8,128)}) %reduce-scatter.6.cloned.1.call-update) | async-done | bytes 16400 | tf_op jit(solution)/shard_map/reduce_scatter | solution.py:54
  320.0 0.8 multiply_reduce_fusion.2
  320.9 105.7 %psum.45 = f32[16]{0:T(128)S(1)} all-reduce(f32[16]{0:T(128)S(1)} %get-tuple-element.10), channel_id=1, replica_groups=mesh['dom'=64,'sub'=8] {'dom','sub'}, use_global_device_ids=true, to_apply=%region_9.10 | all-reduce | flops 16 | bytes 128 | tf_op jit(solution)/shard_map/psum | solution.py:58
  426.8 99.4 %psum.46 = f32[16]{0:T(128)S(1)} all-reduce(f32[16]{0:T(128)S(1)} %get-tuple-element.8), channel_id=1, replica_groups=mesh['dom'=64,'sub'=8] {'dom','sub'}, use_global_device_ids=true, to_apply=%region_11.12 | all-reduce | flops 16 | bytes 128 | tf_op jit(solution)/shard_map/psum | solution.py:31
  527.3 3.9 all-to-all-start.2
  531.7 2.7 collective-permute-start.5
  534.7 1.8 all-to-all-done.2
  536.5 1.3 collective-permute-start.4
  537.8 0.7 copy_add_fusion
  538.5 4.0 collective-permute-done.4
  543.6 29.8 %reduce-scatter.8.cloned.1.call-done = f32[2,16,128]{2,1,0:T(8,128)} async-done(((f32[16,16,128]{2,1,0:T(8,128)}), f32[2,16,128]{2,1,0:T(8,128)}) %reduce-scatter.8.cloned.1.call-update) | async-done | bytes 16400 | tf_op jit(solution)/shard_map/reduce_scatter | solution.py:54
  573.4 0.8 multiply_reduce_fusion
  574.2 105.7 %psum.47 = f32[16]{0:T(128)S(1)} all-reduce(f32[16]{0:T(128)S(1)} %get-tuple-element.6), channel_id=1, replica_groups=mesh['dom'=64,'sub'=8] {'dom','sub'}, use_global_device_ids=true, to_apply=%region_14.15 | all-reduce | flops 16 | bytes 128 | tf_op jit(solution)/shard_map/psum | solution.py:58
  679.9 0.7 multiply_subtract_fusion
  (61 shorter events, 9.5 us)
Async XLA Ops:
  7.2 11.8 %copy-start = (f32[2,4,128,128]{3,2,1,0:T(8,128)S(1)}, f32[2,4,128,128]{3,2,1,0:T(8,128)}, u32[]{:S(2)}) copy-start(f32[2,4,128,128]{3,2,1,0:T(8,128)} %param.8) | copy-start | bytes 1572868
  8.6 10.3 %copy-start.5 = (s32[2]{0:T(128)S(1)}, s32[2]{0:T(128)}, u32[]{:S(2)}) copy-start(s32[2]{0:T(128)} %param.10) | copy-start | bytes 28
  8.6 10.4 %copy-start.2 = (f32[2,16,128]{2,1,0:T(8,128)S(1)}, f32[2,16,128]{2,1,0:T(8,128)}, u32[]{:S(2)}) copy-start(f32[2,16,128]{2,1,0:T(8,128)} %param.6) | copy-start | bytes 49156
  8.6 15.6 %all-to-all-start = ((f32[16,16,128]{2,1,0:T(8,128)}), f32[16,16,128]{2,1,0:T(8,128)S(1)}, u32[]{:S(2)}, u32[]{:S(2)}) async-start(f32[16,16,128]{2,1,0:T(8,128)} %bitcast.2), calls=%async_computation | async-start | bytes 262144 | tf_op jit(solution)/shard_map/all_to_all | solution.py:44
  18.9 0.7 copy-start.3
  18.9 47.8 %reduce-scatter.4.cloned.1.call-start = ((), (), s32[]{:S(2)}) async-start(), calls=%async_computation.6 | async-start | bytes 147456 | tf_op jit(solution)/shard_map/reduce_scatter | solution.py:54
  19.6 0.7 copy-start.4
  20.7 1.4 copy-start.1
  20.8 4.7 collective-permute-start.1
  24.2 6.0 collective-permute-start
  273.9 9.2 %all-to-all-start.1 = ((f32[16,16,128]{2,1,0:T(8,128)}), f32[16,16,128]{2,1,0:T(8,128)S(1)}, u32[]{:S(2)}, u32[]{:S(2)}) async-start(f32[16,16,128]{2,1,0:T(8,128)} %bitcast.12), calls=%async_computation.2 | async-start | bytes 262144 | tf_op jit(solution)/shard_map/all_to_all | solution.py:44
  277.9 42.1 %reduce-scatter.6.cloned.1.call-start = ((), (), s32[]{:S(2)}) async-start(), calls=%async_computation.7 | async-start | bytes 147456 | tf_op jit(solution)/shard_map/reduce_scatter | solution.py:54
  278.4 6.1 collective-permute-start.3
  283.2 6.0 collective-permute-start.2
  527.3 9.2 %all-to-all-start.2 = ((f32[16,16,128]{2,1,0:T(8,128)}), f32[16,16,128]{2,1,0:T(8,128)S(1)}, u32[]{:S(2)}, u32[]{:S(2)}) async-start(f32[16,16,128]{2,1,0:T(8,128)} %bitcast.21), calls=%async_computation.4 | async-start | bytes 262144 | tf_op jit(solution)/shard_map/all_to_all | solution.py:44
  531.2 42.2 %reduce-scatter.8.cloned.1.call-start = ((), (), s32[]{:S(2)}) async-start(), calls=%async_computation.8 | async-start | bytes 147456 | tf_op jit(solution)/shard_map/reduce_scatter | solution.py:54
  531.7 6.1 collective-permute-start.5
  536.5 6.0 collective-permute-start.4
Sparse Core Ops, SparseCore 0:
  26.3 40.2 reduce-scatter.3
  285.3 34.6 reduce-scatter.5
  538.6 34.6 reduce-scatter.7
